TPU v7x, 32 devices: a whole 2x2x4 slice. The times are simulated.
32 devices in a mesh: cfg: 2 (over core), seq: 4 (over z), blk: 4 (over y, x).
Axes of the slice: x: 2, y: 2, z: 4, core: 2. Of those that a mesh axis runs over, the one named last changes fastest.
Arguments:
- img_hidden: bfloat16 [2, 2, 2048, 1536], P('cfg', None, 'seq', 'blk'), may hold values from -15 to 15
- txt_hidden: bfloat16 [2, 2, 160, 1536], P('cfg', None, 'seq', 'blk'), may hold values from -6 to 6
- img_mod: float32 [2, 2, 6, 1536], P('cfg'), may hold values from -9 to 9
- txt_mod: float32 [2, 2, 2, 1536], P('cfg'), may hold values from -3 to 3
- out_mod: float32 [2, 2, 2, 1536], P('cfg'), may hold values from -3 to 3
- w_qkv: bfloat16 [3, 1536, 1536], P(None, None, 'blk'), may hold values from -0.25 to 0.25
- w_txt_kv: bfloat16 [2, 1536, 1536], P(None, None, 'blk'), may hold values from -0.25 to 0.25
- w_out: bfloat16 [1536, 1536], P('blk'), may hold values from -0.15625 to 0.15625
- w_fc1: bfloat16 [1536, 6144], P(None, 'blk'), may hold values from -0.15625 to 0.15625
- w_fc2: bfloat16 [6144, 1536], P('blk'), may hold values from -0.078125 to 0.078125
- w_proj: bfloat16 [1536, 64], P('blk'), may hold values from -0.15625 to 0.15625
- latent: float32 [2, 2048, 64], P(None, 'seq', 'cfg'), may hold values from -6 to 6
- lengths: int32 [2, 2], P('cfg'), may hold values from 1 to 154, as said below
- t_index: int32 [2], replicated, may hold values from 0 to 24
- stride: int32 [2], replicated, may hold values from 1 to 4
- guide: float32 [2], replicated, may hold values from 4 to 8
Outputs:
- new_latent: float32 [2, 2048, 64], P(None, 'seq', 'cfg')
- update_max: float32 [2], replicated
Inputs may be any that keep to these rules, and one draw needn't show every extreme that they name: `lengths`: at least one entry equals 154.
All inputs are finite; a program needn't handle non-finite values.
Results may differ from a plain program's by a relative error of at most 0.015.
Values may be sent and summed in bfloat16 or wider, within the bound.
A program may use at most 192 MiB of HBM per device.

v0:
```python
import jax
import jax.numpy as jnp
from jax import lax
from jax.sharding import PartitionSpec as P

HEAD = 64
STEPS = 28
EPSILON = 1e-06
BLOCK_ROWS = 512


def from_partner(value, axis, bit):
    return lax.ppermute(value, axis, [(i, i ^ 1 << bit) for i in range(lax.axis_size(axis))])


def normalize(values):
    values = values.astype(jnp.float32)
    center = jnp.mean(values, axis=-1, keepdims=True)
    spread = jnp.mean(jnp.square(values - center), axis=-1, keepdims=True)
    return (values - center) * lax.rsqrt(spread + EPSILON)


def modulate(values, scale_row, shift_row):
    return (normalize(values) * (1.0 + scale_row[:, None, :]) + shift_row[:, None, :]).astype(
        jnp.bfloat16
    )


def project(values, weight):
    flat_rows = values.reshape(-1, values.shape[-1])
    result = jnp.dot(flat_rows, weight, preferred_element_type=jnp.float32)
    return result.reshape(values.shape[:-1] + (weight.shape[-1],))


def noise_level(step_index):
    remain = 1.0 - step_index.astype(jnp.float32) / STEPS
    return 3.0 * remain / (1.0 + 2.0 * remain)


def own_columns(values, column_block, shard_width):
    return lax.dynamic_slice_in_dim(
        values, column_block * shard_width, shard_width, values.ndim - 1
    )


def per_device(
    img_hidden,
    txt_hidden,
    img_mod,
    txt_mod,
    out_mod,
    w_qkv,
    w_txt_kv,
    w_out,
    w_fc1,
    w_fc2,
    w_proj,
    latent,
    lengths,
    t_index,
    stride,
    guide,
):
    column_block = lax.axis_index("blk")
    shard_width = img_hidden.shape[3]
    model_width = shard_width * lax.axis_size("blk")
    image_full, text_full = (
        lax.all_gather(img_hidden[0], "blk", axis=2, tiled=True),
        lax.all_gather(txt_hidden[0], "blk", axis=2, tiled=True),
    )
    image_mod = img_mod[0]
    prompts = image_full.shape[0]
    img_rows = image_full.shape[1]
    attn_in = modulate(image_full, image_mod[:, 1], image_mod[:, 0])
    queries = project(attn_in, w_qkv[0]).astype(jnp.bfloat16)
    keys_img = project(attn_in, w_qkv[1]).astype(jnp.bfloat16)
    values_img = project(attn_in, w_qkv[2]).astype(jnp.bfloat16)
    text_norm = modulate(text_full, txt_mod[0][:, 0], txt_mod[0][:, 1])
    text_keys = project(text_norm, w_txt_kv[0]).astype(jnp.bfloat16)
    text_values = project(text_norm, w_txt_kv[1]).astype(jnp.bfloat16)
    head_width = queries.shape[2]
    head_count = head_width // HEAD
    query_heads = queries.reshape(prompts, img_rows, head_count, HEAD)
    text_limit = lengths[0]

    def attend_block(running_state, key_block, value_block, live_mask):
        accumulated, running, denominator = running_state
        key_count = key_block.shape[1]
        key_heads = key_block.reshape(prompts, key_count, head_count, HEAD)
        value_heads = value_block.reshape(prompts, key_count, head_count, HEAD)
        scores = jnp.einsum(
            "pqhe,pkhe->phqk", query_heads, key_heads, preferred_element_type=jnp.float32
        ) * HEAD ** (-0.5)
        if live_mask is not None:
            scores = jnp.where(live_mask[:, None, None, :], scores, -jnp.inf)
        updated = jnp.maximum(running, jnp.max(scores, axis=-1))
        factor = jnp.exp(running - updated)
        weights = jnp.exp(scores - updated[..., None])
        denominator = denominator * factor + jnp.sum(weights, axis=-1)
        mixed_values = jnp.einsum(
            "phqk,pkhe->phqe",
            weights.astype(jnp.bfloat16),
            value_heads,
            preferred_element_type=jnp.float32,
        )
        accumulated = accumulated * factor[..., None] + mixed_values
        return (accumulated, updated, denominator)

    initial = (
        jnp.zeros((prompts, head_count, img_rows, HEAD), jnp.float32),
        jnp.full((prompts, head_count, img_rows), -1e30, jnp.float32),
        jnp.zeros((prompts, head_count, img_rows), jnp.float32),
    )
    running_state = initial
    key_piece = lax.all_gather(keys_img, "seq", axis=1, tiled=True)
    value_piece = lax.all_gather(values_img, "seq", axis=1, tiled=True)
    key_count = key_piece.shape[1]
    blocks = key_count // BLOCK_ROWS
    key_split = key_piece.reshape(prompts, blocks, BLOCK_ROWS, head_width).transpose(1, 0, 2, 3)
    value_split = value_piece.reshape(prompts, blocks, BLOCK_ROWS, head_width).transpose(1, 0, 2, 3)

    def scan_step(state_now, operands):
        key_block, value_block = operands
        return (attend_block(state_now, key_block, value_block, None), None)

    running_state, unused = lax.scan(scan_step, running_state, (key_split, value_split))
    all_text_keys, all_text_values = (
        lax.all_gather(text_keys, "seq", axis=1, tiled=True),
        lax.all_gather(text_values, "seq", axis=1, tiled=True),
    )
    slot_index = jnp.arange(all_text_keys.shape[1], dtype=jnp.int32)
    text_mask = slot_index[None, :] < text_limit[:, None]
    accumulated, running, denominator = attend_block(
        running_state, all_text_keys, all_text_values, text_mask
    )
    attended = (accumulated / denominator[..., None]).astype(jnp.bfloat16)
    attended = attended.transpose(0, 2, 1, 3).reshape(prompts, img_rows, head_width)
    attn_part = project(attended, w_out)
    attn_sum = lax.psum(attn_part.astype(jnp.bfloat16), "blk").astype(jnp.float32)
    resid_full = (image_full.astype(jnp.float32) + image_mod[:, 2][:, None, :] * attn_sum).astype(
        jnp.bfloat16
    )
    resid_one = own_columns(resid_full, column_block, shard_width)
    mlp_in = modulate(resid_full, image_mod[:, 4], image_mod[:, 3])
    hidden_units = jax.nn.gelu(project(mlp_in, w_fc1), approximate=True).astype(jnp.bfloat16)
    mlp_sum = lax.psum_scatter(
        project(hidden_units, w_fc2).astype(jnp.bfloat16), "blk", scatter_dimension=2, tiled=True
    ).astype(jnp.float32)
    gate_mlp = own_columns(image_mod[:, 5], column_block, shard_width)
    resid_two = (resid_one.astype(jnp.float32) + gate_mlp[:, None, :] * mlp_sum).astype(
        jnp.bfloat16
    )
    stream = resid_two.astype(jnp.float32)
    row_sum, row_squares = lax.psum(
        (jnp.sum(stream, axis=-1), jnp.sum(stream * stream, axis=-1)), "blk"
    )
    center = row_sum / model_width
    spread = row_squares / model_width - center * center
    final_mod = out_mod[0]
    final_scale = own_columns(final_mod[:, 0], column_block, shard_width)
    final_shift = own_columns(final_mod[:, 1], column_block, shard_width)
    final_in = (
        (stream - center[..., None])
        * lax.rsqrt(spread[..., None] + EPSILON)
        * (1.0 + final_scale[:, None, :])
        + final_shift[:, None, :]
    ).astype(jnp.bfloat16)
    velocity_part = project(final_in, w_proj)
    half_index = lax.axis_index("cfg")
    channel_width = latent.shape[2]
    guide_scale = guide[:, None, None]
    velocity = lax.psum(velocity_part.astype(jnp.bfloat16), "blk").astype(jnp.float32)
    outgoing = own_columns(velocity, 1 - half_index, channel_width)
    other_half = from_partner(outgoing.astype(jnp.bfloat16), "cfg", 0).astype(outgoing.dtype)
    own_half = own_columns(velocity, half_index, channel_width)
    velocity_cond = jnp.where(half_index == 0, own_half, other_half)
    velocity_uncond = jnp.where(half_index == 0, other_half, own_half)
    guided = velocity_uncond + guide_scale * (velocity_cond - velocity_uncond)
    step_size = noise_level(t_index + stride) - noise_level(t_index)
    update = step_size[:, None, None] * guided
    new_latent = latent + update
    local_peak = jnp.max(jnp.abs(update), axis=(1, 2))
    peak_value = lax.pmax(local_peak, ("cfg", "seq"))
    return (new_latent, peak_value)


def solution(mesh):
    placed = (
        P("cfg", None, "seq", "blk"),
        P("cfg", None, "seq", "blk"),
        P("cfg", None, None, None),
        P("cfg", None, None, None),
        P("cfg", None, None, None),
        P(None, None, "blk"),
        P(None, None, "blk"),
        P("blk", None),
        P(None, "blk"),
        P("blk", None),
        P("blk", None),
        P(None, "seq", "cfg"),
        P("cfg", None),
        P(),
        P(),
        P(),
    )
    return jax.shard_map(
        per_device,
        mesh=mesh,
        in_specs=placed,
        out_specs=(P(None, "seq", "cfg"), P()),
        check_vma=False,
    )
```

profile of v0, /device:TPU:0, one launch (start us, length us, event | category | flops | bytes accessed | tf_op | source)
XLA Modules:
  0.0 552.0 jit_solution(2850391820597721948)
XLA Ops:
  9.6 46.8 %all-gather.10.cloned.1.call-done = bf16[1,2,512,1536]{3,2,1,0:T(8,128)(2,1)} async-done(((bf16[1,2,512,384]{3,2,1,0:T(8,128)(2,1)}), bf16[1,2,512,1536]{3,2,1,0:T(8,128)(2,1)}) %all-gather.10.cloned.1.call-update) | async-done | bytes 3145744 | tf_op jit(solution)/shard_map/all_gather | solution.py:68
  64.4 5.0 convolution_convert_fusion.3
  69.5 9.2 %all-gather.1 = bf16[1,2,40,1536]{3,2,1,0:T(8,128)(2,1)S(1)} all-gather(bf16[1,2,40,384]{3,2,1,0:T(8,128)(2,1)S(1)} %copy-done.12), channel_id=3, replica_groups=mesh['cfg'=2,'seq'=4,'blk'=4] {'blk'}, dimensions={3}, use_global_device_ids=true | all-gather | bytes 307200 | tf_op jit(solution)/shard_map/all_gather | solution.py:69
  80.8 16.4 %all_gather.22 = bf16[2,160,384]{2,1,0:T(8,128)(2,1)} all-gather(bf16[2,40,384]{2,1,0:T(8,128)(2,1)S(1)} %fusion.79), channel_id=1, replica_groups=mesh['cfg'=2,'seq'=4,'blk'=4] {'seq'}, dimensions={1}, use_global_device_ids=true | all-gather | bytes 307200 | tf_op jit(solution)/shard_map/all_gather | solution.py:128
  100.0 16.7 %all_gather.23 = bf16[2,160,384]{2,1,0:T(8,128)(2,1)S(1)} all-gather(bf16[2,40,384]{2,1,0:T(8,128)(2,1)S(1)} %fusion.82), channel_id=1, replica_groups=mesh['cfg'=2,'seq'=4,'blk'=4] {'seq'}, dimensions={1}, use_global_device_ids=true | all-gather | bytes 307200 | tf_op jit(solution)/shard_map/all_gather | solution.py:129
  125.9 9.6 %all-gather.8.cloned.1.call-done = bf16[2,2048,384]{2,1,0:T(8,128)(2,1)} async-done(((bf16[2,512,384]{2,1,0:T(8,128)(2,1)}), bf16[2,2048,384]{2,1,0:T(8,128)(2,1)}) %all-gather.8.cloned.1.call-update) | async-done | bytes 3145744 | tf_op jit(solution)/shard_map/all_gather | solution.py:116
  140.2 59.2 %all-gather.6.cloned.1.call-done = bf16[2,2048,384]{2,1,0:T(8,128)(2,1)} async-done(((bf16[2,512,384]{2,1,0:T(8,128)(2,1)}), bf16[2,2048,384]{2,1,0:T(8,128)(2,1)}) %all-gather.6.cloned.1.call-update) | async-done | bytes 3145744 | tf_op jit(solution)/shard_map/all_gather | solution.py:115
  199.4 4.7 copy.36
  204.1 87.5 %while.15 = (s32[]{:T(128)}, f32[2,6,512,64]{2,3,1,0:T(8,128)S(1)}, f32[2,6,512]{2,1,0:T(8,128)}, f32[2,6,512]{2,1,0:T(8,128)}, bf16[4,2,512,384]{2,3,1,0:T(8,12...) while((s32[]{:T(128)}, f32[2,6,512,64]{2,3,1,0:T(8,128)S(1)}, ...), condition=%wide.region_5.0_spmd.clone, body=%wide.region_2.5_spmd.clone.sunk | while | flops 831682560 | bytes 97419496 | solution.py:126
  205.5 8.1 %bitcast_reduce_fusion.2 = (f32[2,6,512]{2,1,0:T(8,128)}, f32[2,6,512,512]{3,2,1,0:T(8,128)}) fusion(bf16[2,512,6,64]{1,3,2,0:T(8,128)(2,1)S(1)} %bitcast.165, bf16[2,512,6,64]{1,3,2,0:T(8,128)(2,1)} %get-tuple-element.199), kind=kOutput, calls=%fused_computation.1.clone.1 | convolution fusion | flops 408938496 | bytes 14180352 | tf_op jit(solution)/shard_map/while/body/eval_jaxpr/pqhe,pkhe->phqk/dot_general | solution.py:91
  214.4 6.8 %fusion.134 = f32[2,6,512]{2,1,0:T(8,128)S(1)} fusion(f32[2,6,512,512]{3,2,1,0:T(8,128)} %get-tuple-element.172, f32[2,6,512]{2,1,0:T(8,128)S(1)} %select_maximum_fusion.2), kind=kLoop, calls=%fused_computation.3.clone.1 | loop fusion | flops 9431040 | bytes 12632064 | tf_op jit(solution)/shard_map/while/body/eval_jaxpr/reduce_sum | solution.py:99
  227.4 8.1 %bitcast_reduce_fusion.2 = (f32[2,6,512]{2,1,0:T(8,128)}, f32[2,6,512,512]{3,2,1,0:T(8,128)}) fusion(bf16[2,512,6,64]{1,3,2,0:T(8,128)(2,1)S(1)} %bitcast.165, bf16[2,512,6,64]{1,3,2,0:T(8,128)(2,1)} %get-tuple-element.199), kind=kOutput, calls=%fused_computation.1.clone.1 | convolution fusion | flops 408938496 | bytes 14180352 | tf_op jit(solution)/shard_map/while/body/eval_jaxpr/pqhe,pkhe->phqk/dot_general | solution.py:91
  236.3 6.8 %fusion.134 = f32[2,6,512]{2,1,0:T(8,128)S(1)} fusion(f32[2,6,512,512]{3,2,1,0:T(8,128)} %get-tuple-element.172, f32[2,6,512]{2,1,0:T(8,128)S(1)} %select_maximum_fusion.2), kind=kLoop, calls=%fused_computation.3.clone.1 | loop fusion | flops 9431040 | bytes 12632064 | tf_op jit(solution)/shard_map/while/body/eval_jaxpr/reduce_sum | solution.py:99
  249.3 8.1 %bitcast_reduce_fusion.2 = (f32[2,6,512]{2,1,0:T(8,128)}, f32[2,6,512,512]{3,2,1,0:T(8,128)}) fusion(bf16[2,512,6,64]{1,3,2,0:T(8,128)(2,1)S(1)} %bitcast.165, bf16[2,512,6,64]{1,3,2,0:T(8,128)(2,1)} %get-tuple-element.199), kind=kOutput, calls=%fused_computation.1.clone.1 | convolution fusion | flops 408938496 | bytes 14180352 | tf_op jit(solution)/shard_map/while/body/eval_jaxpr/pqhe,pkhe->phqk/dot_general | solution.py:91
  258.2 6.8 %fusion.134 = f32[2,6,512]{2,1,0:T(8,128)S(1)} fusion(f32[2,6,512,512]{3,2,1,0:T(8,128)} %get-tuple-element.172, f32[2,6,512]{2,1,0:T(8,128)S(1)} %select_maximum_fusion.2), kind=kLoop, calls=%fused_computation.3.clone.1 | loop fusion | flops 9431040 | bytes 12632064 | tf_op jit(solution)/shard_map/while/body/eval_jaxpr/reduce_sum | solution.py:99
  271.2 8.1 %bitcast_reduce_fusion.2 = (f32[2,6,512]{2,1,0:T(8,128)}, f32[2,6,512,512]{3,2,1,0:T(8,128)}) fusion(bf16[2,512,6,64]{1,3,2,0:T(8,128)(2,1)S(1)} %bitcast.165, bf16[2,512,6,64]{1,3,2,0:T(8,128)(2,1)} %get-tuple-element.199), kind=kOutput, calls=%fused_computation.1.clone.1 | convolution fusion | flops 408938496 | bytes 14180352 | tf_op jit(solution)/shard_map/while/body/eval_jaxpr/pqhe,pkhe->phqk/dot_general | solution.py:91
  280.1 6.8 %fusion.134 = f32[2,6,512]{2,1,0:T(8,128)S(1)} fusion(f32[2,6,512,512]{3,2,1,0:T(8,128)} %get-tuple-element.172, f32[2,6,512]{2,1,0:T(8,128)S(1)} %select_maximum_fusion.2), kind=kLoop, calls=%fused_computation.3.clone.1 | loop fusion | flops 9431040 | bytes 12632064 | tf_op jit(solution)/shard_map/while/body/eval_jaxpr/reduce_sum | solution.py:99
  301.8 85.9 %all-reduce.4.cloned.1.call-done = bf16[2,512,1536]{2,1,0:T(8,128)(2,1)} async-done(((bf16[2,512,1536]{2,1,0:T(8,128)(2,1)}), bf16[2,512,1536]{2,1,0:T(8,128)(2,1)}) %all-reduce.4.cloned.1.call-update) | async-done | bytes 3145744 | tf_op jit(solution)/shard_map/psum | solution.py:139
  394.4 15.8 %fusion.38 = bf16[2,512,1536]{2,1,0:T(8,128)(2,1)} fusion(bf16[1536,1536]{1,0:T(8,128)(2,1)} %param.27, bf16[1536,1536]{1,0:T(8,128)(2,1)} %param.26, bf16[2,512,1536]{2,1,0:T(8,128)(2,1)} %copy-done.4, f32[2,1536]{1,0:T(2,128)S(1)} %get-tuple-element.113, f32[2,1536]{1,0:T(2,128)S(1)} %get-tuple-element.114, f32[2,512]{1,0:T(2,128)S(1)} %add_rsqrt_fusion.1, ...), kind=kOutput, calls=%fused_computation.50 | convolution fusion | flops 9688842240 | bytes 15761408 | tf_op jit(solution)/shard_map/dot_general | solution.py:31
  410.2 8.7 %copy.44 = bf16[2,512,1536]{1,0,2:T(2,128)(2,1)} copy(bf16[2,512,1536]{2,1,0:T(8,128)(2,1)} %fusion.38) | data formatting | bytes 6291456
  424.2 43.3 %reduce-scatter.4.cloned.1.call-done = bf16[384,1024]{1,0:T(8,128)(2,1)} async-done(((bf16[1536,1024]{1,0:T(8,128)(2,1)}), bf16[384,1024]{1,0:T(8,128)(2,1)}) %reduce-scatter.4.cloned.1.call-update) | async-done | bytes 786448
  472.4 9.1 %all-reduce = (f32[2,512]{1,0:T(2,128)S(1)}, f32[2,512]{1,0:T(2,128)S(1)}) all-reduce(f32[2,512]{1,0:T(2,128)S(1)} %get-tuple-element.69, f32[2,512]{1,0:T(2,128)S(1)} %get-tuple-element.68), channel_id=1, replica_groups=mesh['cfg'=2,'seq'=4,'blk'=4] {'blk'}, use_global_device_ids=true, to_apply=%region_17.18 | all-reduce | flops 2048 | bytes 16384 | tf_op jit(solution)/shard_map/psum | solution.py:154
  482.7 42.1 %all-reduce.6.cloned.1.call-done = bf16[2,512,64]{1,2,0:T(8,128)(2,1)} async-done(((bf16[2,512,64]{1,2,0:T(8,128)(2,1)}), bf16[2,512,64]{1,2,0:T(8,128)(2,1)}) %all-reduce.6.cloned.1.call-update) | async-done | bytes 131088 | tf_op jit(solution)/shard_map/psum | solution.py:172
  527.9 17.2 %pmax.7 = f32[2]{0:T(128)} all-reduce(f32[2]{0:T(128)S(1)} %get-tuple-element.97), channel_id=1, replica_groups=mesh['cfg'=2,'seq'=4,'blk'=4] {'cfg','seq'}, use_global_device_ids=true, to_apply=%region_20.21 | all-reduce | flops 2 | bytes 16 | tf_op jit(solution)/shard_map/pmax | solution.py:183
  (154 shorter events, 87.8 us)
Async XLA Ops:
  7.2 291.0 %copy-start = (bf16[384,1536]{1,0:T(8,128)(2,1)S(1)}, bf16[384,1536]{1,0:T(8,128)(2,1)}, u32[]{:S(2)}) copy-start(bf16[384,1536]{1,0:T(8,128)(2,1)} %param.25) | copy-start | bytes 3538948
  7.2 49.2 %all-gather.10.cloned.1.call-start = ((), (), s32[]{:S(2)}) async-start(), calls=%async_computation.5 | async-start | bytes 3932160 | tf_op jit(solution)/shard_map/all_gather | solution.py:68
  7.9 127.6 %all-gather.8.cloned.1.call-start = ((), (), s32[]{:S(2)}) async-start(), calls=%async_computation.2 | async-start | bytes 3932160 | tf_op jit(solution)/shard_map/all_gather | solution.py:116
  64.3 14.7 %copy-start.15 = (f32[1,2,2,1536]{3,2,1,0:T(2,128)S(1)}, f32[1,2,2,1536]{3,2,1,0:T(2,128)}, u32[]{:S(2)}) copy-start(f32[1,2,2,1536]{3,2,1,0:T(2,128)} %param.21) | copy-start | bytes 73732
  64.3 135.0 %all-gather.6.cloned.1.call-start = ((), (), s32[]{:S(2)}) async-start(), calls=%async_computation.1 | async-start | bytes 3932160 | tf_op jit(solution)/shard_map/all_gather | solution.py:115
  69.3 48.2 %copy-start.19 = (s32[1,2]{1,0:T(1,128)S(1)}, s32[1,2]{1,0:T(1,128)}, u32[]{:S(2)}) copy-start(s32[1,2]{1,0:T(1,128)} %param.30) | copy-start | bytes 28
  69.4 318.3 %all-reduce.4.cloned.1.call-start = ((), (), s32[]{:S(2)}) async-start(), calls=%async_computation.3 | async-start | bytes 6291456 | tf_op jit(solution)/shard_map/psum | solution.py:139
  214.4 6.9 %copy-start.6 = (f32[2,6,512]{2,1,0:T(8,128)S(1)}, f32[2,6,512]{2,1,0:T(8,128)}, u32[]{:S(2)}) copy-start(f32[2,6,512]{2,1,0:T(8,128)} %get-tuple-element.187) | copy-start | bytes 73732 | tf_op jit(solution)/shard_map/while
  214.4 6.9 %copy-start.8 = (f32[2,6,512]{2,1,0:T(8,128)S(1)}, f32[2,6,512]{2,1,0:T(8,128)}, u32[]{:S(2)}) copy-start(f32[2,6,512]{2,1,0:T(8,128)} %get-tuple-element.188) | copy-start | bytes 73732 | tf_op jit(solution)/shard_map/while
  214.4 8.2 %copy-start.1 = (f32[2,6,512,512]{3,2,1,0:T(8,128)S(1)}, f32[2,6,512,512]{3,2,1,0:T(8,128)}, u32[]{:S(2)}) copy-start(f32[2,6,512,512]{3,2,1,0:T(8,128)} %get-tuple-element.172) | copy-start | bytes 37748740 | tf_op jit(solution)/shard_map/while
  236.3 6.9 %copy-start.8 = (f32[2,6,512]{2,1,0:T(8,128)S(1)}, f32[2,6,512]{2,1,0:T(8,128)}, u32[]{:S(2)}) copy-start(f32[2,6,512]{2,1,0:T(8,128)} %get-tuple-element.188) | copy-start | bytes 73732 | tf_op jit(solution)/shard_map/while
  236.3 8.2 %copy-start.1 = (f32[2,6,512,512]{3,2,1,0:T(8,128)S(1)}, f32[2,6,512,512]{3,2,1,0:T(8,128)}, u32[]{:S(2)}) copy-start(f32[2,6,512,512]{3,2,1,0:T(8,128)} %get-tuple-element.172) | copy-start | bytes 37748740 | tf_op jit(solution)/shard_map/while
  258.2 6.9 %copy-start.8 = (f32[2,6,512]{2,1,0:T(8,128)S(1)}, f32[2,6,512]{2,1,0:T(8,128)}, u32[]{:S(2)}) copy-start(f32[2,6,512]{2,1,0:T(8,128)} %get-tuple-element.188) | copy-start | bytes 73732 | tf_op jit(solution)/shard_map/while
  258.2 8.2 %copy-start.1 = (f32[2,6,512,512]{3,2,1,0:T(8,128)S(1)}, f32[2,6,512,512]{3,2,1,0:T(8,128)}, u32[]{:S(2)}) copy-start(f32[2,6,512,512]{3,2,1,0:T(8,128)} %get-tuple-element.172) | copy-start | bytes 37748740 | tf_op jit(solution)/shard_map/while
  280.1 6.9 %copy-start.8 = (f32[2,6,512]{2,1,0:T(8,128)S(1)}, f32[2,6,512]{2,1,0:T(8,128)}, u32[]{:S(2)}) copy-start(f32[2,6,512]{2,1,0:T(8,128)} %get-tuple-element.188) | copy-start | bytes 73732 | tf_op jit(solution)/shard_map/while
  280.1 8.2 %copy-start.1 = (f32[2,6,512,512]{3,2,1,0:T(8,128)S(1)}, f32[2,6,512,512]{3,2,1,0:T(8,128)}, u32[]{:S(2)}) copy-start(f32[2,6,512,512]{3,2,1,0:T(8,128)} %get-tuple-element.172) | copy-start | bytes 37748740 | tf_op jit(solution)/shard_map/while
  301.7 165.8 %reduce-scatter.4.cloned.1.call-start = ((), (), s32[]{:S(2)}) async-start(), calls=%async_computation.6 | async-start | bytes 3932160
  423.3 58.2 %copy-start.18 = (bf16[384,64]{0,1:T(8,128)(2,1)S(1)}, bf16[384,64]{0,1:T(8,128)(2,1)}, u32[]{:S(2)}) copy-start(bf16[384,64]{0,1:T(8,128)(2,1)} %param.28) | copy-start | bytes 147460
  423.3 101.5 %all-reduce.6.cloned.1.call-start = ((), (), s32[]{:S(2)}) async-start(), calls=%async_computation.4 | async-start | bytes 262144 | tf_op jit(solution)/shard_map/psum | solution.py:172
  424.1 101.7 %copy-start.20 = (s32[2]{0:T(128)S(1)}, s32[2]{0:T(128)}, u32[]{:S(2)}) copy-start(s32[2]{0:T(128)} %param.31) | copy-start | bytes 28
  424.2 101.7 %copy-start.21 = (s32[2]{0:T(128)S(1)}, s32[2]{0:T(128)}, u32[]{:S(2)}) copy-start(s32[2]{0:T(128)} %param.32) | copy-start | bytes 28
  424.2 103.0 %copy-start.11 = (f32[2,512,32]{1,2,0:T(8,128)S(1)}, f32[2,512,32]{1,2,0:T(8,128)}, u32[]{:S(2)}) copy-start(f32[2,512,32]{1,2,0:T(8,128)} %param.29) | copy-start | bytes 393220
  424.2 102.9 %copy-start.17 = (f32[2]{0:T(128)S(1)}, f32[2]{0:T(128)}, u32[]{:S(2)}) copy-start(f32[2]{0:T(128)} %param.33) | copy-start | bytes 28
  525.8 1.3 collective-permute-start
  (17 other events, 72.4 us)
Sparse Core Ops, SparseCore 0:
  9.8 46.5 all-gather.9
  64.4 71.0 all-gather.7
  137.1 62.2 all-gather.5
  301.8 85.8 all-reduce.3
  423.4 43.9 reduce-scatter.3
  482.9 41.9 all-reduce.5
where the time goes:
time: 553 us; the launch traced here: 552 us
  waiting for transfers between devices  289 us (52%)
  matrix products  85.7 us (15%)
  blocking collectives  68.6 us (12%)
  other arithmetic  47.8 us (9%)
  local copies, waits for them, and re-layouts  45.9 us (8%)
  between operations  14.5 us (3%)
    psum x1, waiting for transfers between devices, per_device(): lax.psum(attn_part.astype(jnp.bfloat16), 'blk').astype(jnp.float32)  85.9 us
    all_gather x1, waiting for transfers between devices, per_device(): key_piece = lax.all_gather(keys_img, 'seq', axis=1, tiled=True)  59.2 us
    all_gather x1, waiting for transfers between devices, per_device(): lax.all_gather(img_hidden[0], 'blk', axis=2, tiled=True)  46.8 us
    unnamed x7, waiting for transfers between devices  44 us
    psum x1, waiting for transfers between devices, per_device(): lax.psum(velocity_part.astype(jnp.bfloat16), 'blk').astype(jnp.float32)  42.1 us
    dot_general x8, matrix products, project(): result = jnp.dot(flat_rows, weight, preferred_element_type=jnp.float32)  37 us
    dot_general x5, matrix products, attend_block(): jnp.einsum('pqhe,pkhe->phqk', query_heads, key_heads, preferred_element_t...  35.9 us
    reduce_sum x5, other arithmetic, attend_block(): denominator = denominator * factor + jnp.sum(weights, axis=-1)  30.6 us
  transfers between devices with their start and end apart: 7, of which 7 were waited for; matrix products, arithmetic and copies ran while one was open for 5% of the time, Pallas kernels for 0%

commit v1 on v0

--- a/solution.py
+++ b/solution.py
@@ -61,6 +61,20 @@
     stride,
     guide,
 ):
+
+    def link_clusters(a0, device_axis):
+        newest = lax.axis_size(device_axis)
+        fresh = lax.axis_index(device_axis)
+        z1, block_next, now = (newest, fresh, a0.shape[1])
+        finding, v1 = (a0, 1)
+        while v1 < z1:
+            mid_arr = map(lambda it: (it, (it - v1) % z1), range(z1))
+            current_arr = list(mid_arr)
+            new = lax.ppermute(finding, device_axis, current_arr)
+            finding = jnp.concatenate([finding, new], 1)
+            v1 = 2 * v1
+        return jnp.roll(finding, shift=block_next * now, axis=1)
+
     column_block = lax.axis_index("blk")
     shard_width = img_hidden.shape[3]
     model_width = shard_width * lax.axis_size("blk")
@@ -125,7 +139,7 @@
 
     running_state, unused = lax.scan(scan_step, running_state, (key_split, value_split))
     all_text_keys, all_text_values = (
-        lax.all_gather(text_keys, "seq", axis=1, tiled=True),
+        link_clusters(text_keys, "seq"),
         lax.all_gather(text_values, "seq", axis=1, tiled=True),
     )
     slot_index = jnp.arange(all_text_keys.shape[1], dtype=jnp.int32)

time: 553 us -> 556 us (level)
  blocking collectives: 68.6 us -> 62.6 us
    all_gather x1, waiting for transfers between devices: 59.2 us -> 8.01 us  [per_device(): key_piece = lax.all_gather(keys_img, 'seq', axis=1, tiled=True)]
    all_gather x1, waiting for transfers between devices: 9.59 us -> 59 us  [per_device(): value_piece = lax.all_gather(values_img, 'seq', axis=1, tiled=True)]
    all_gather x1 -> x0, blocking collectives: 16.4 us -> none  [per_device(): lax.all_gather(text_keys, 'seq', axis=1, tiled=True)]
    all_gather x1, blocking collectives: 16.7 us -> 27 us  [per_device(): lax.all_gather(text_values, 'seq', axis=1, tiled=True)]
    unnamed x48 -> x52, local copies, waits for them, and re-layouts: 20.2 us -> 22.8 us
  transfers between devices with their start and end apart: 7 -> 9, of which waited for: 7 -> 8; matrix products, arithmetic and copies ran while one was open for 5% -> 5% of each run, Pallas kernels for 0% -> 0%
where the time goes in v1:
time: 556 us; the launch traced here: 554 us
  waiting for transfers between devices  289 us (52%)
  matrix products  86.4 us (16%)
  blocking collectives  62.6 us (11%)
  local copies, waits for them, and re-layouts  49.2 us (9%)
  other arithmetic  47.8 us (9%)
  between operations  14.5 us (3%)
    psum x1, waiting for transfers between devices, per_device(): lax.psum(attn_part.astype(jnp.bfloat16), 'blk').astype(jnp.float32)  85.9 us
    all_gather x1, waiting for transfers between devices, per_device(): value_piece = lax.all_gather(values_img, 'seq', axis=1, tiled=True)  59 us
    all_gather x1, waiting for transfers between devices, per_device(): lax.all_gather(img_hidden[0], 'blk', axis=2, tiled=True)  46.8 us
    unnamed x7, waiting for transfers between devices  44 us
    psum x1, waiting for transfers between devices, per_device(): lax.psum(velocity_part.astype(jnp.bfloat16), 'blk').astype(jnp.float32)  42.1 us
    dot_general x8, matrix products, project(): result = jnp.dot(flat_rows, weight, preferred_element_type=jnp.float32)  37.7 us
    dot_general x5, matrix products, attend_block(): jnp.einsum('pqhe,pkhe->phqk', query_heads, key_heads, preferred_element_t...  35.8 us
    reduce_sum x5, other arithmetic, attend_block(): denominator = denominator * factor + jnp.sum(weights, axis=-1)  30.6 us
  transfers between devices with their start and end apart: 9, of which 8 were waited for; matrix products, arithmetic and copies ran while one was open for 5% of the time, Pallas kernels for 0%

profile of v1, /device:TPU:0, one launch (start us, length us, event | category | flops | bytes accessed | tf_op | source)
XLA Modules:
  0.0 554.4 jit_solution(5784932743576147067)
XLA Ops:
  9.6 46.8 %all-gather.10.cloned.1.call-done = bf16[1,2,512,1536]{3,2,1,0:T(8,128)(2,1)} async-done(((bf16[1,2,512,384]{3,2,1,0:T(8,128)(2,1)}), bf16[1,2,512,1536]{3,2,1,0:T(8,128)(2,1)}) %all-gather.10.cloned.1.call-update) | async-done | bytes 3145744 | tf_op jit(solution)/shard_map/all_gather | solution.py:82
  64.4 5.0 convolution_convert_fusion.1
  69.4 9.2 %all-gather.1 = bf16[1,2,40,1536]{3,2,1,0:T(8,128)(2,1)S(1)} all-gather(bf16[1,2,40,384]{3,2,1,0:T(8,128)(2,1)S(1)} %copy-done.12), channel_id=3, replica_groups=mesh['cfg'=2,'seq'=4,'blk'=4] {'blk'}, dimensions={3}, use_global_device_ids=true | all-gather | bytes 307200 | tf_op jit(solution)/shard_map/all_gather | solution.py:83
  89.4 27.0 %all_gather.19 = bf16[2,160,384]{2,1,0:T(8,128)(2,1)S(1)} all-gather(bf16[2,40,384]{2,1,0:T(8,128)(2,1)S(1)} %fusion.82), channel_id=1, replica_groups=mesh['cfg'=2,'seq'=4,'blk'=4] {'seq'}, dimensions={1}, use_global_device_ids=true | all-gather | bytes 307200 | tf_op jit(solution)/shard_map/all_gather | solution.py:143
  130.1 8.0 %all-gather.6.cloned.1.call-done = bf16[2,2048,384]{2,1,0:T(8,128)(2,1)} async-done(((bf16[2,512,384]{2,1,0:T(8,128)(2,1)}), bf16[2,2048,384]{2,1,0:T(8,128)(2,1)}) %all-gather.6.cloned.1.call-update) | async-done | bytes 3145744 | tf_op jit(solution)/shard_map/all_gather | solution.py:129
  138.1 4.7 copy.35
  142.8 59.0 %all-gather.8.cloned.1.call-done = bf16[2,2048,384]{2,1,0:T(8,128)(2,1)} async-done(((bf16[2,512,384]{2,1,0:T(8,128)(2,1)}), bf16[2,2048,384]{2,1,0:T(8,128)(2,1)}) %all-gather.8.cloned.1.call-update) | async-done | bytes 3145744 | tf_op jit(solution)/shard_map/all_gather | solution.py:130
  201.8 4.7 copy.37
  206.5 87.5 %while.15 = (s32[]{:T(128)}, f32[2,6,512,64]{2,3,1,0:T(8,128)S(1)}, f32[2,6,512]{2,1,0:T(8,128)}, f32[2,6,512]{2,1,0:T(8,128)}, bf16[4,2,512,384]{2,3,1,0:T(8,12...) while((s32[]{:T(128)}, f32[2,6,512,64]{2,3,1,0:T(8,128)S(1)}, ...), condition=%wide.region_5.0_spmd.clone, body=%wide.region_2.5_spmd.clone.sunk | while | flops 831682560 | bytes 97419496 | solution.py:140
  208.0 8.1 %bitcast_reduce_fusion.2 = (f32[2,6,512]{2,1,0:T(8,128)}, f32[2,6,512,512]{3,2,1,0:T(8,128)}) fusion(bf16[2,512,6,64]{1,3,2,0:T(8,128)(2,1)S(1)} %bitcast.169, bf16[2,512,6,64]{1,3,2,0:T(8,128)(2,1)} %get-tuple-element.201), kind=kOutput, calls=%fused_computation.1.clone.1 | convolution fusion | flops 408938496 | bytes 14180352 | tf_op jit(solution)/shard_map/while/body/eval_jaxpr/pqhe,pkhe->phqk/dot_general | solution.py:105
  216.9 6.8 %fusion.134 = f32[2,6,512]{2,1,0:T(8,128)S(1)} fusion(f32[2,6,512,512]{3,2,1,0:T(8,128)} %get-tuple-element.174, f32[2,6,512]{2,1,0:T(8,128)S(1)} %select_maximum_fusion.2), kind=kLoop, calls=%fused_computation.3.clone.1 | loop fusion | flops 9431040 | bytes 12632064 | tf_op jit(solution)/shard_map/while/body/eval_jaxpr/reduce_sum | solution.py:113
  229.9 8.1 %bitcast_reduce_fusion.2 = (f32[2,6,512]{2,1,0:T(8,128)}, f32[2,6,512,512]{3,2,1,0:T(8,128)}) fusion(bf16[2,512,6,64]{1,3,2,0:T(8,128)(2,1)S(1)} %bitcast.169, bf16[2,512,6,64]{1,3,2,0:T(8,128)(2,1)} %get-tuple-element.201), kind=kOutput, calls=%fused_computation.1.clone.1 | convolution fusion | flops 408938496 | bytes 14180352 | tf_op jit(solution)/shard_map/while/body/eval_jaxpr/pqhe,pkhe->phqk/dot_general | solution.py:105
  238.8 6.8 %fusion.134 = f32[2,6,512]{2,1,0:T(8,128)S(1)} fusion(f32[2,6,512,512]{3,2,1,0:T(8,128)} %get-tuple-element.174, f32[2,6,512]{2,1,0:T(8,128)S(1)} %select_maximum_fusion.2), kind=kLoop, calls=%fused_computation.3.clone.1 | loop fusion | flops 9431040 | bytes 12632064 | tf_op jit(solution)/shard_map/while/body/eval_jaxpr/reduce_sum | solution.py:113
  251.8 8.1 %bitcast_reduce_fusion.2 = (f32[2,6,512]{2,1,0:T(8,128)}, f32[2,6,512,512]{3,2,1,0:T(8,128)}) fusion(bf16[2,512,6,64]{1,3,2,0:T(8,128)(2,1)S(1)} %bitcast.169, bf16[2,512,6,64]{1,3,2,0:T(8,128)(2,1)} %get-tuple-element.201), kind=kOutput, calls=%fused_computation.1.clone.1 | convolution fusion | flops 408938496 | bytes 14180352 | tf_op jit(solution)/shard_map/while/body/eval_jaxpr/pqhe,pkhe->phqk/dot_general | solution.py:105
  260.7 6.8 %fusion.134 = f32[2,6,512]{2,1,0:T(8,128)S(1)} fusion(f32[2,6,512,512]{3,2,1,0:T(8,128)} %get-tuple-element.174, f32[2,6,512]{2,1,0:T(8,128)S(1)} %select_maximum_fusion.2), kind=kLoop, calls=%fused_computation.3.clone.1 | loop fusion | flops 9431040 | bytes 12632064 | tf_op jit(solution)/shard_map/while/body/eval_jaxpr/reduce_sum | solution.py:113
  273.6 8.1 %bitcast_reduce_fusion.2 = (f32[2,6,512]{2,1,0:T(8,128)}, f32[2,6,512,512]{3,2,1,0:T(8,128)}) fusion(bf16[2,512,6,64]{1,3,2,0:T(8,128)(2,1)S(1)} %bitcast.169, bf16[2,512,6,64]{1,3,2,0:T(8,128)(2,1)} %get-tuple-element.201), kind=kOutput, calls=%fused_computation.1.clone.1 | convolution fusion | flops 408938496 | bytes 14180352 | tf_op jit(solution)/shard_map/while/body/eval_jaxpr/pqhe,pkhe->phqk/dot_general | solution.py:105
  282.6 6.8 %fusion.134 = f32[2,6,512]{2,1,0:T(8,128)S(1)} fusion(f32[2,6,512,512]{3,2,1,0:T(8,128)} %get-tuple-element.174, f32[2,6,512]{2,1,0:T(8,128)S(1)} %select_maximum_fusion.2), kind=kLoop, calls=%fused_computation.3.clone.1 | loop fusion | flops 9431040 | bytes 12632064 | tf_op jit(solution)/shard_map/while/body/eval_jaxpr/reduce_sum | solution.py:113
  304.2 85.9 %all-reduce.4.cloned.1.call-done = bf16[2,512,1536]{2,1,0:T(8,128)(2,1)} async-done(((bf16[2,512,1536]{2,1,0:T(8,128)(2,1)}), bf16[2,512,1536]{2,1,0:T(8,128)(2,1)}) %all-reduce.4.cloned.1.call-update) | async-done | bytes 3145744 | tf_op jit(solution)/shard_map/psum | solution.py:153
  396.8 15.9 %fusion.38 = bf16[2,512,1536]{2,1,0:T(8,128)(2,1)} fusion(bf16[1536,1536]{1,0:T(8,128)(2,1)} %param.27, bf16[1536,1536]{1,0:T(8,128)(2,1)} %param.26, bf16[2,512,1536]{2,1,0:T(8,128)(2,1)} %copy-done.4, f32[2,1536]{1,0:T(2,128)S(1)} %get-tuple-element.115, f32[2,1536]{1,0:T(2,128)S(1)} %get-tuple-element.116, f32[2,512]{1,0:T(2,128)S(1)} %add_rsqrt_fusion.1, ...), kind=kOutput, calls=%fused_computation.50 | convolution fusion | flops 9688842240 | bytes 15761408 | tf_op jit(solution)/shard_map/dot_general | solution.py:31
  412.7 8.6 %copy.43 = bf16[2,512,1536]{1,0,2:T(2,128)(2,1)} copy(bf16[2,512,1536]{2,1,0:T(8,128)(2,1)} %fusion.38) | data formatting | bytes 6291456
  426.7 43.2 %reduce-scatter.4.cloned.1.call-done = bf16[384,1024]{1,0:T(8,128)(2,1)} async-done(((bf16[1536,1024]{1,0:T(8,128)(2,1)}), bf16[384,1024]{1,0:T(8,128)(2,1)}) %reduce-scatter.4.cloned.1.call-update) | async-done | bytes 786448
  474.9 9.1 %all-reduce = (f32[2,512]{1,0:T(2,128)S(1)}, f32[2,512]{1,0:T(2,128)S(1)}) all-reduce(f32[2,512]{1,0:T(2,128)S(1)} %get-tuple-element.69, f32[2,512]{1,0:T(2,128)S(1)} %get-tuple-element.68), channel_id=1, replica_groups=mesh['cfg'=2,'seq'=4,'blk'=4] {'blk'}, use_global_device_ids=true, to_apply=%region_17.18 | all-reduce | flops 2048 | bytes 16384 | tf_op jit(solution)/shard_map/psum | solution.py:168
  485.2 42.1 %all-reduce.6.cloned.1.call-done = bf16[2,512,64]{1,2,0:T(8,128)(2,1)} async-done(((bf16[2,512,64]{1,2,0:T(8,128)(2,1)}), bf16[2,512,64]{1,2,0:T(8,128)(2,1)}) %all-reduce.6.cloned.1.call-update) | async-done | bytes 131088 | tf_op jit(solution)/shard_map/psum | solution.py:186
  530.4 17.2 %pmax.7 = f32[2]{0:T(128)} all-reduce(f32[2]{0:T(128)S(1)} %get-tuple-element.97), channel_id=1, replica_groups=mesh['cfg'=2,'seq'=4,'blk'=4] {'cfg','seq'}, use_global_device_ids=true, to_apply=%region_20.21 | all-reduce | flops 2 | bytes 16 | tf_op jit(solution)/shard_map/pmax | solution.py:197
  (164 shorter events, 93.3 us)
Async XLA Ops:
  7.2 293.4 %copy-start = (bf16[384,1536]{1,0:T(8,128)(2,1)S(1)}, bf16[384,1536]{1,0:T(8,128)(2,1)}, u32[]{:S(2)}) copy-start(bf16[384,1536]{1,0:T(8,128)(2,1)} %param.25) | copy-start | bytes 3538948
  7.2 49.2 %all-gather.10.cloned.1.call-start = ((), (), s32[]{:S(2)}) async-start(), calls=%async_computation.5 | async-start | bytes 3932160 | tf_op jit(solution)/shard_map/all_gather | solution.py:82
  7.9 130.2 %all-gather.6.cloned.1.call-start = ((), (), s32[]{:S(2)}) async-start(), calls=%async_computation.1 | async-start | bytes 3932160 | tf_op jit(solution)/shard_map/all_gather | solution.py:129
  64.3 14.7 %copy-start.15 = (f32[1,2,2,1536]{3,2,1,0:T(2,128)S(1)}, f32[1,2,2,1536]{3,2,1,0:T(2,128)}, u32[]{:S(2)}) copy-start(f32[1,2,2,1536]{3,2,1,0:T(2,128)} %param.21) | copy-start | bytes 73732
  64.3 137.5 %all-gather.8.cloned.1.call-start = ((), (), s32[]{:S(2)}) async-start(), calls=%async_computation.2 | async-start | bytes 3932160 | tf_op jit(solution)/shard_map/all_gather | solution.py:130
  69.3 17.1 %copy-start.19 = (s32[1,2]{1,0:T(1,128)S(1)}, s32[1,2]{1,0:T(1,128)}, u32[]{:S(2)}) copy-start(s32[1,2]{1,0:T(1,128)} %param.30) | copy-start | bytes 28
  69.4 320.8 %all-reduce.4.cloned.1.call-start = ((), (), s32[]{:S(2)}) async-start(), calls=%async_computation.3 | async-start | bytes 6291456 | tf_op jit(solution)/shard_map/psum | solution.py:153
  81.4 6.9 %collective-permute-start = (bf16[2,40,384]{2,1,0:T(8,128)(2,1)S(1)}, bf16[2,40,384]{2,1,0:T(8,128)(2,1)S(1)}, u32[]{:S(2)}, u32[]{:S(2)}) collective-permute-start(bf16[2,40,384]{2,1,0:T(8,128)(2,1)S(1)} %get-tuple-element.112), channel_id=1, source_target_pairs={{0,12},{4,0},{8,4},{12,8},{1,13},{5,1},{9,5},{13,9},{2,14},{6,2},{... | collective-permute-start | bytes 184328 | tf_op jit(solution)/shard_map/ppermute | solution.py:73
  88.2 29.7 %collective-permute-start.1 = (bf16[2,80,384]{2,1,0:T(8,128)(2,1)S(1)}, bf16[2,80,384]{2,1,0:T(8,128)(2,1)S(1)}, u32[]{:S(2)}, u32[]{:S(2)}) collective-permute-start(bf16[2,80,384]{2,1,0:T(8,128)(2,1)S(1)} %pad_maximum_fusion), channel_id=1, source_target_pairs={{0,8},{4,12},{8,0},{12,4},{1,9},{5,13},{9,1},{13,5},{2,10},{6,14},... | collective-permute-start | bytes 368648 | tf_op jit(solution)/shard_map/ppermute | solution.py:73
  216.9 6.9 %copy-start.8 = (f32[2,6,512]{2,1,0:T(8,128)S(1)}, f32[2,6,512]{2,1,0:T(8,128)}, u32[]{:S(2)}) copy-start(f32[2,6,512]{2,1,0:T(8,128)} %get-tuple-element.190) | copy-start | bytes 73732 | tf_op jit(solution)/shard_map/while
  216.9 8.2 %copy-start.1 = (f32[2,6,512,512]{3,2,1,0:T(8,128)S(1)}, f32[2,6,512,512]{3,2,1,0:T(8,128)}, u32[]{:S(2)}) copy-start(f32[2,6,512,512]{3,2,1,0:T(8,128)} %get-tuple-element.174) | copy-start | bytes 37748740 | tf_op jit(solution)/shard_map/while
  238.8 6.9 %copy-start.8 = (f32[2,6,512]{2,1,0:T(8,128)S(1)}, f32[2,6,512]{2,1,0:T(8,128)}, u32[]{:S(2)}) copy-start(f32[2,6,512]{2,1,0:T(8,128)} %get-tuple-element.190) | copy-start | bytes 73732 | tf_op jit(solution)/shard_map/while
  238.8 8.2 %copy-start.1 = (f32[2,6,512,512]{3,2,1,0:T(8,128)S(1)}, f32[2,6,512,512]{3,2,1,0:T(8,128)}, u32[]{:S(2)}) copy-start(f32[2,6,512,512]{3,2,1,0:T(8,128)} %get-tuple-element.174) | copy-start | bytes 37748740 | tf_op jit(solution)/shard_map/while
  260.7 6.9 %copy-start.8 = (f32[2,6,512]{2,1,0:T(8,128)S(1)}, f32[2,6,512]{2,1,0:T(8,128)}, u32[]{:S(2)}) copy-start(f32[2,6,512]{2,1,0:T(8,128)} %get-tuple-element.190) | copy-start | bytes 73732 | tf_op jit(solution)/shard_map/while
  260.7 8.2 %copy-start.1 = (f32[2,6,512,512]{3,2,1,0:T(8,128)S(1)}, f32[2,6,512,512]{3,2,1,0:T(8,128)}, u32[]{:S(2)}) copy-start(f32[2,6,512,512]{3,2,1,0:T(8,128)} %get-tuple-element.174) | copy-start | bytes 37748740 | tf_op jit(solution)/shard_map/while
  282.5 8.2 %copy-start.1 = (f32[2,6,512,512]{3,2,1,0:T(8,128)S(1)}, f32[2,6,512,512]{3,2,1,0:T(8,128)}, u32[]{:S(2)}) copy-start(f32[2,6,512,512]{3,2,1,0:T(8,128)} %get-tuple-element.174) | copy-start | bytes 37748740 | tf_op jit(solution)/shard_map/while
  304.1 165.8 %reduce-scatter.4.cloned.1.call-start = ((), (), s32[]{:S(2)}) async-start(), calls=%async_computation.6 | async-start | bytes 3932160
  425.8 58.2 %copy-start.18 = (bf16[384,64]{0,1:T(8,128)(2,1)S(1)}, bf16[384,64]{0,1:T(8,128)(2,1)}, u32[]{:S(2)}) copy-start(bf16[384,64]{0,1:T(8,128)(2,1)} %param.28) | copy-start | bytes 147460
  425.8 101.5 %all-reduce.6.cloned.1.call-start = ((), (), s32[]{:S(2)}) async-start(), calls=%async_computation.4 | async-start | bytes 262144 | tf_op jit(solution)/shard_map/psum | solution.py:186
  426.6 101.7 %copy-start.20 = (s32[2]{0:T(128)S(1)}, s32[2]{0:T(128)}, u32[]{:S(2)}) copy-start(s32[2]{0:T(128)} %param.31) | copy-start | bytes 28
  426.6 101.7 %copy-start.21 = (s32[2]{0:T(128)S(1)}, s32[2]{0:T(128)}, u32[]{:S(2)}) copy-start(s32[2]{0:T(128)} %param.32) | copy-start | bytes 28
  426.7 102.9 %copy-start.11 = (f32[2,512,32]{1,2,0:T(8,128)S(1)}, f32[2,512,32]{1,2,0:T(8,128)}, u32[]{:S(2)}) copy-start(f32[2,512,32]{1,2,0:T(8,128)} %param.29) | copy-start | bytes 393220
  426.7 102.9 %copy-start.17 = (f32[2]{0:T(128)S(1)}, f32[2]{0:T(128)}, u32[]{:S(2)}) copy-start(f32[2]{0:T(128)} %param.33) | copy-start | bytes 28
  528.3 1.3 collective-permute-start.2
  (19 other events, 86.1 us)
Sparse Core Ops, SparseCore 0:
  9.8 46.5 all-gather.9
  64.4 73.6 all-gather.5
  139.7 62.1 all-gather.7
  304.3 85.8 all-reduce.3
  425.9 43.9 reduce-scatter.3
  485.3 41.9 all-reduce.5
